TPU v7x, 32 devices: a whole 2x2x4 slice. The times are simulated.
32 devices in a mesh: tile: 8 (over z, y), band: 4 (over x, core).
Axes of the slice: x: 2, y: 2, z: 4, core: 2. Of those that a mesh axis runs over, the one named last changes fastest.
Arguments:
- sky_model: bfloat16 [4, 16384, 128], P('band', 'tile'), may hold values from -6 to 6
- observed: bfloat16 [4, 8, 1024, 128], P('band', 'tile'), may hold values from -6 to 6
- row_weight: float32 [4, 8, 128], P('band', 'tile'), may hold values from 0.1 to 1
- foot_owner: int32 [4, 8, 1024, 1], P('band', 'tile'), may hold values from 0 to 7; in each aligned block of 1024 rows (0 to 1023, 1024 to 2047, ..., all dimensions but the last counted through in order) at most 256 rows name the same one
- foot_local: int32 [4, 8, 1024], P('band', 'tile'), may hold values from 0 to 2047
- row_offset: int32 [4, 8], P('band', 'tile'), may hold values from -4 to 4
- exposure_of: int32 [4, 8], P('band', 'tile'), may hold values from 0 to 255
- amplitude: float32 [4, 256], replicated, may hold values from 0.25 to 1
- subpixel_shift: float32 [256], replicated, may hold values from 0.05 to 0.95
- column_profile: float32 [256, 4, 25], replicated, may hold values from 0.05 to 0.3
- row_profile: float32 [256, 4, 25], replicated, may hold values from 0.05 to 0.3
Outputs:
- grad_sky: float32 [4, 16384, 128], P('band', 'tile')
- grad_params: float32 [5, 256], replicated
Inputs may be any that keep to these rules, and one draw needn't show every extreme that they name: `foot_owner`: in each aligned block of 1024 columns (the columns of one device's row blocks) no owner index appears more than 256 times, and some owner appears exactly 256 times in some blocks.
All inputs are finite; a program needn't handle non-finite values.
Results may differ from a plain program's by a relative error of at most 0.006.
Values may be sent and summed in bfloat16 or wider, within the bound.
A program may use at most 64 MiB of HBM per device.

v0:
```python
import functools

import jax
import jax.numpy as jnp
from jax import lax
from jax.experimental import pallas as pl
from jax.experimental.pallas import tpu as pltpu
from jax.sharding import PartitionSpec as P

MESH = pl.DeviceIdType.MESH
BF = jnp.bfloat16
F32 = jnp.float32
TN = (((0,), (0,)), ((), ()))
NT = (((1,), (1,)), ((), ()))


def iota(shape, dim):
    return lax.broadcasted_iota(jnp.int32, shape, dim)


def dot(a, b):
    return jnp.dot(a, b, preferred_element_type=F32)


def onehot(hit):
    return jnp.where(hit, 1.0, 0.0).astype(BF)


def spread(ref, expo):
    taps, comps, expos = ref.shape
    named = iota((comps, expos), 1) == expo
    lane = iota((comps, 256), 1) - (128 - taps // 2)
    straight = mirrored = jnp.zeros((comps, 256), F32)
    for t in range(taps):
        tap = jnp.sum(jnp.where(named, ref[t], 0.0), axis=1, keepdims=True)
        straight = jnp.where(lane == t, tap, straight)
        mirrored = jnp.where(lane == taps - 1 - t, tap, mirrored)
    return straight.astype(BF).astype(F32), mirrored.astype(BF).astype(F32)


def bands(base):
    x = jnp.concatenate([base] * 16, axis=0)
    row = iota(x.shape, 0)
    for bit in range(7):
        x = jnp.where((row & (1 << bit)) != 0, pltpu.roll(x, 1 << bit, 1), x)
    return x


def kernel(
    tiles,
    nband,
    cap,
    owner_ref,
    local_ref,
    weight_ref,
    offset_ref,
    expo_ref,
    amp_ref,
    frac_ref,
    sky_hbm,
    obs_hbm,
    col_hbm,
    rowp_hbm,
    total,
    summed_ref,
    sky,
    sky_t,
    obs,
    colp,
    rowp,
    hits,
    picks,
    req_out,
    req_in,
    rows_out,
    rows_in,
    grads_out,
    grads_in,
    card_out,
    cards,
    part_out,
    part_in,
    fet,
    resam,
    base,
    blur,
    fwd,
    bwd,
    tall,
    tall_t,
    obs_t,
    resid,
    back,
    adj,
    seg_grad,
    load_sem,
    req_s,
    req_r,
    rows_s,
    rows_r,
    grads_s,
    grads_r,
    cards_s,
    cards_r,
    part_s,
    part_r,
):
    me = lax.axis_index("tile")
    band = lax.axis_index("band")
    segs, rows = sky.shape
    width = obs.shape[0]
    comps = blur.shape[0]
    pixels = width * rows
    nblk = width // 256
    half = tiles // 2

    loads = [
        pltpu.make_async_copy(src, dst, load_sem.at[i])
        for i, (src, dst) in enumerate(
            ((sky_hbm, sky), (obs_hbm, obs), (col_hbm, colp), (rowp_hbm, rowp))
        )
    ]
    for load in loads:
        load.start()

    barrier = pltpu.get_barrier_semaphore()

    def loop(low, high, work):
        lax.fori_loop(low, high, lambda k, c: (work(k), c)[1], 0)

    loop(
        1,
        tiles,
        lambda k: pl.semaphore_signal(
            barrier, inc=1, device_id={"tile": lax.rem(me + k, tiles)}, device_id_type=MESH
        ),
    )
    loop(
        1,
        nband,
        lambda k: pl.semaphore_signal(
            barrier, inc=1, device_id={"band": lax.rem(band + k, nband)}, device_id_type=MESH
        ),
    )

    def after(step):
        return lax.rem(me + 1 + step, tiles)

    def ahead(step):
        return lax.rem(me + 2 * tiles - 1 - step, tiles)

    def push(src, dst, send, recv, p):
        return pltpu.make_async_remote_copy(
            src_ref=src.at[p],
            dst_ref=dst.at[me],
            send_sem=send.at[p],
            recv_sem=recv.at[me],
            device_id={"tile": p},
            device_id_type=MESH,
        )

    def arrival(src, dst, send, recv, p):
        return pltpu.make_async_remote_copy(
            src_ref=src.at[p],
            dst_ref=dst.at[p],
            send_sem=send.at[p],
            recv_sem=recv.at[p],
            device_id={"tile": p},
            device_id_type=MESH,
        )

    def deliver(src, dst, send, recv, p):
        @pl.when(p != me)
        def _():
            push(src, dst, send, recv, p).start()

        @pl.when(p == me)
        def _():
            dst[me] = src[me]

    def receive(src, dst, send, recv, p):
        @pl.when(p != me)
        def _():
            arrival(src, dst, send, recv, p).wait_recv()

    owner = owner_ref[...]
    member = jnp.where(iota((tiles, width), 0) == owner, 1.0, 0.0)
    pieces = [member[:, b * 128 : (b + 1) * 128] for b in range(width // 128)]
    above = onehot(iota((128, 128), 0) < iota((128, 128), 1))
    prefix = dot(jnp.concatenate(pieces, axis=0).astype(BF), above)
    run = jnp.zeros((tiles, 1), F32)
    ranks = []
    for b, piece in enumerate(pieces):
        earlier = prefix[b * tiles : (b + 1) * tiles] + run
        ranks.append(jnp.sum(piece * earlier, axis=0, keepdims=True))
        run = run + jnp.sum(piece, axis=1, keepdims=True)
    slot = owner * cap + jnp.concatenate(ranks, axis=1).astype(jnp.int32)
    wanted = local_ref[...] + 1
    which = iota((16, width), 0)
    digits = (
        jnp.where(which == 0, wanted >> 6, jnp.where(which == 1, wanted & 63, 0))
        .astype(F32)
        .astype(BF)
    )
    pl.semaphore_wait(barrier, tiles - 1 + nband - 1)

    def ask(step):
        p = after(step)
        hit = onehot(iota((cap, width), 0) + p * cap == slot)
        hits[p] = hit
        ids = lax.dot_general(digits, hit, NT, preferred_element_type=F32)
        req_out[p] = ids[0:1] * 64.0 + ids[1:2]
        deliver(req_out, req_in, req_s, req_r, p)

    loop(0, tiles, ask)
    loads[0].wait()
    for b in range(segs // 128):
        sky_t[:, b * 128 : (b + 1) * 128] = sky[b * 128 : (b + 1) * 128, :].T

    keep = cap >= 128

    def pick(p):
        return onehot(iota((segs, cap), 0) + 1 == req_in[p].astype(jnp.int32))

    def serve(step):
        p = ahead(step)
        receive(req_out, req_in, req_s, req_r, p)
        chosen = pick(p)
        if keep:
            picks[p] = chosen
        rows_out[p] = dot(sky_t[...], chosen).astype(BF)
        deliver(rows_out, rows_in, rows_s, rows_r, p)

    loop(0, tiles, serve)

    for load in loads[1:]:
        load.wait()
    expo = expo_ref[0, 0]
    offset = offset_ref[0, 0]
    amps = [amp_ref[q, expo] for q in range(comps)]
    for at, made in enumerate((*spread(colp, expo), *spread(rowp, expo))):
        for q in range(comps):
            base[at, q] = jnp.broadcast_to(made[q : q + 1], (8, 256))
    low = iota((128, 128), 1) < 64
    blank = jnp.zeros((128, 128), BF)

    def make_wide(at, wide):
        def work(q):
            made = bands(base[at, q])
            edge, mid = made[:, :128], made[:, 128:].astype(BF)
            left = jnp.where(low, 0.0, edge).astype(BF)
            right = jnp.where(low, edge, 0.0).astype(BF)
            for b, line in enumerate(((right, blank), (mid, right), (left, mid), (blank, left))):
                for h in range(2):
                    wide[q, b * 128 : (b + 1) * 128, h * 128 : (h + 1) * 128] = line[h]

        loop(0, comps, work)

    make_wide(1, fwd)
    make_wide(0, bwd)

    def make_tall(q):
        tall[q] = bands(base[2, q])[:, 128:].astype(BF)
        tall_t[q] = bands(base[3, q])[:, 128:].astype(BF)
        blur[q, :, :128] = blank
        blur[q, :, 128 + width :] = blank

    loop(0, comps, make_tall)
    resid[:, :128] = blank
    resid[:, 128 + width :] = blank
    for b in range(width // 128):
        obs_t[:, b * 128 : (b + 1) * 128] = obs[b * 128 : (b + 1) * 128, :].T
    heavy = jnp.broadcast_to(weight_ref[...], (128, 128)).T
    heavy = jnp.concatenate([heavy, heavy], axis=1)
    frac = jnp.full((128, 128), frac_ref[expo], F32)
    w_low = (1.0 - frac).astype(BF).astype(F32)
    w_high = frac.astype(BF).astype(F32)
    sub, lane = iota((128, 128), 0), iota((128, 128), 1)
    interp_t = (
        jnp.where(lane == sub + offset, w_low, 0.0)
        + jnp.where(lane == sub + offset + 1, w_high, 0.0)
    ).astype(BF)
    interp = (
        jnp.where(sub == lane + offset, w_low, 0.0)
        + jnp.where(sub == lane + offset + 1, w_high, 0.0)
    ).astype(BF)
    slope_t = (
        jnp.where(lane == sub + offset + 1, 1.0, 0.0) - jnp.where(lane == sub + offset, 1.0, 0.0)
    ).astype(BF)

    fet[...] = jnp.zeros_like(fet)

    def take(step):
        p = after(step)
        receive(rows_out, rows_in, rows_s, rows_r, p)
        fet[...] += dot(rows_in[p], hits[p])

    loop(0, tiles, take)

    resam[...] = dot(interp_t, fet[...].astype(BF)).astype(BF)

    tall_rows = jnp.concatenate([tall[q] for q in range(comps)], axis=0)
    for i in range(nblk):
        part = dot(tall_rows, resam[:, i * 256 : (i + 1) * 256])
        for q in range(comps):
            blur[q, :, 128 + i * 256 : 384 + i * 256] = (
                amps[q] * part[q * 128 : (q + 1) * 128]
            ).astype(BF)

    for i in range(nblk):
        model = None
        for q in range(comps):
            part = dot(blur[q, :, i * 256 : i * 256 + 512], fwd[q])
            model = part if model is None else model + part
        weighted = heavy * (model - obs_t[:, i * 256 : (i + 1) * 256].astype(F32))
        resid[:, 128 + i * 256 : 384 + i * 256] = weighted.astype(BF)
    tall_all = jnp.concatenate([tall_t[q] for q in range(comps)], axis=1)
    for i in range(nblk):
        left = resid[:, i * 256 : i * 256 + 512]
        stack = []
        for q in range(comps):
            part = amps[q] * dot(left, bwd[q])
            back[q, :, i * 256 : (i + 1) * 256] = part
            stack.append(part.astype(BF))
        adjoint = dot(tall_all, jnp.concatenate(stack, axis=0))
        adj[:, i * 256 : (i + 1) * 256] = adjoint
        seg_grad[:, i * 256 : (i + 1) * 256] = dot(interp, adjoint.astype(BF)).astype(BF)

    def give(step):
        p = after(step)
        sent = lax.dot_general(seg_grad[...], hits[p], NT, preferred_element_type=F32)
        grads_out[p] = sent.astype(BF)
        deliver(grads_out, grads_in, grads_s, grads_r, p)

    loop(0, half, give)

    terms = []
    for q in range(comps):
        acc = jnp.sum(blur[q, :, 128 : 128 + width].astype(F32) * back[q], axis=0, keepdims=True)
        gain = jnp.full((1, 1), amps[q], F32)
        terms.append(jnp.sum(acc, axis=1, keepdims=True) / (gain * gain * pixels))
    shift = jnp.sum(adj[...] * dot(slope_t, fet[...].astype(BF)), axis=0, keepdims=True)
    terms.append(jnp.sum(shift, axis=1, keepdims=True) / pixels)

    line = iota((8, 128), 0)
    card = jnp.where(line == 5, expo.astype(F32), 0.0)
    for q, term in enumerate(terms):
        card = jnp.where(line == q, jnp.broadcast_to(term, (8, 128)), card)
    card_out[...] = card
    cards[band] = card

    def swap(k, here):
        to = lax.rem(band + k, nband)
        return pltpu.make_async_remote_copy(
            src_ref=card_out,
            dst_ref=cards.at[band] if here else cards.at[to],
            send_sem=cards_s.at[to],
            recv_sem=cards_r.at[band] if here else cards_r.at[to],
            device_id={"band": to},
            device_id_type=MESH,
        )

    loop(1, nband, lambda k: swap(k, True).start())

    loop(half, tiles, give)

    loop(1, nband, lambda k: swap(k, False).wait_recv())
    expos = summed_ref.shape[1]
    column = iota((8, expos), 1).astype(F32)
    part = jnp.zeros((8, expos), F32)
    for b in range(nband):
        block = jnp.concatenate([cards[b]] * (expos // 128), axis=1)
        part = part + jnp.where(column == block[5:6, :], block, 0.0)
    part_out[...] = part
    part_in[me] = part

    def tell(k, here):
        p = lax.rem(me + k, tiles)
        return pltpu.make_async_remote_copy(
            src_ref=part_out,
            dst_ref=part_in.at[me] if here else part_in.at[p],
            send_sem=part_s.at[p],
            recv_sem=part_r.at[me] if here else part_r.at[p],
            device_id={"tile": p},
            device_id_type=MESH,
        )

    loop(1, tiles, lambda k: tell(k, True).start())

    total[...] = jnp.zeros_like(total)

    def collect(step):
        p = ahead(step)
        receive(grads_out, grads_in, grads_s, grads_r, p)
        chosen = picks[p] if keep else pick(p)
        total[...] += lax.dot_general(chosen, grads_in[p], NT, preferred_element_type=F32)

    loop(0, tiles, collect)

    loop(1, tiles, lambda k: tell(k, False).wait_recv())
    summed = lax.fori_loop(0, tiles, lambda t, acc: acc + part_in[t], jnp.zeros((8, expos), F32))
    summed_ref[...] = summed[: comps + 1]

    def settle(k):
        p = lax.rem(me + k, tiles)
        push(req_out, req_in, req_s, req_r, p).wait_send()
        push(rows_out, rows_in, rows_s, rows_r, p).wait_send()
        push(grads_out, grads_in, grads_s, grads_r, p).wait_send()
        tell(k, True).wait_send()

    loop(1, tiles, settle)
    loop(1, nband, lambda k: swap(k, True).wait_send())


def body(
    sky_model,
    observed,
    row_weight,
    foot_owner,
    foot_local,
    row_offset,
    exposure_of,
    amplitude,
    subpixel_shift,
    column_profile,
    row_profile,
):
    tiles = lax.axis_size("tile")
    nband = lax.axis_size("band")
    segs, rows = sky_model.shape[1:]
    width = observed.shape[2]
    comps, expos = amplitude.shape
    taps = column_profile.shape[2]
    cap = 2 * width // tiles
    vmem = pl.BlockSpec(memory_space=pltpu.VMEM)
    smem = pl.BlockSpec(memory_space=pltpu.SMEM)
    hbm = pl.BlockSpec(memory_space=pltpu.HBM)
    dma = pltpu.SemaphoreType.DMA
    grad, params = pl.pallas_call(
        functools.partial(kernel, tiles, nband, cap),
        out_shape=(
            jax.ShapeDtypeStruct((segs, rows), F32),
            jax.ShapeDtypeStruct((comps + 1, expos), F32),
        ),
        in_specs=[vmem, vmem, vmem, smem, smem, smem, smem, hbm, hbm, hbm, hbm],
        out_specs=(vmem, vmem),
        scratch_shapes=[
            pltpu.VMEM((segs, rows), BF),
            pltpu.VMEM((rows, segs), BF),
            pltpu.VMEM((width, rows), BF),
            pltpu.VMEM((taps, comps, expos), F32),
            pltpu.VMEM((taps, comps, expos), F32),
            pltpu.VMEM((tiles, cap, width), BF),
            pltpu.VMEM((tiles, segs, cap) if cap >= 128 else (16, 128), BF),
            pltpu.VMEM((tiles, 1, cap), F32),
            pltpu.VMEM((tiles, 1, cap), F32),
            pltpu.VMEM((tiles, rows, cap), BF),
            pltpu.VMEM((tiles, rows, cap), BF),
            pltpu.VMEM((tiles, rows, cap), BF),
            pltpu.VMEM((tiles, rows, cap), BF),
            pltpu.VMEM((8, 128), F32),
            pltpu.VMEM((nband, 8, 128), F32),
            pltpu.VMEM((8, expos), F32),
            pltpu.VMEM((tiles, 8, expos), F32),
            pltpu.VMEM((rows, width), F32),
            pltpu.VMEM((rows, width), BF),
            pltpu.VMEM((4, comps, 8, 256), F32),
            pltpu.VMEM((comps, rows, width + 256), BF),
            pltpu.VMEM((comps, 512, 256), BF),
            pltpu.VMEM((comps, 512, 256), BF),
            pltpu.VMEM((comps, rows, rows), BF),
            pltpu.VMEM((comps, rows, rows), BF),
            pltpu.VMEM((rows, width), BF),
            pltpu.VMEM((rows, width + 256), BF),
            pltpu.VMEM((comps, rows, width), F32),
            pltpu.VMEM((rows, width), F32),
            pltpu.VMEM((rows, width), BF),
            dma((4,)),
        ]
        + [dma((tiles,))] * 6
        + [dma((nband,))] * 2
        + [dma((tiles,))] * 2,
        compiler_params=pltpu.CompilerParams(
            collective_id=0, has_side_effects=True, vmem_limit_bytes=60 * 1024 * 1024
        ),
    )(
        foot_owner.reshape(1, width),
        foot_local.reshape(1, width),
        row_weight.reshape(1, rows),
        row_offset,
        exposure_of,
        amplitude,
        subpixel_shift,
        sky_model[0],
        observed[0, 0],
        column_profile.transpose(2, 1, 0),
        row_profile.transpose(2, 1, 0),
    )
    return (grad[None], params)


def solution(mesh):
    placed = (
        P("band", "tile", None),
        P("band", "tile", None, None),
        P("band", "tile", None),
        P("band", "tile", None, None),
        P("band", "tile", None),
        P("band", "tile"),
        P("band", "tile"),
        P(),
        P(),
        P(),
        P(),
    )
    return jax.shard_map(
        body, mesh=mesh, in_specs=placed, out_specs=(P("band", "tile", None), P()), check_vma=False
    )
```

profile of v0, /device:TPU:0, one launch (start us, length us, event | category | flops | bytes accessed | tf_op | source)
XLA Modules:
  0.0 47.6 jit_solution(15522115447941089847)
XLA Ops:
  1.9 42.8 %shard_map.122 = (f32[2048,128]{1,0:T(8,128)}, f32[5,256]{1,0:T(8,128)}) custom-call(s32[1,1024]{1,0:T(1,128)} %bitcast.13, s32[1,1024]{1,0:T(1,128)} %bitcast.14, f32[1,128]{1,0:T(1,128)} %bitcast.15, s32[1,1]{1,0:T(1,128)S(6)} %copy.15.offset_ref, s32[1,1]{1,0:T(1,128)S(6)} %copy.16.expo_ref, f32[4,256]{1,0:T(4,128)} %amp_ref.1, f32[256]{0:T(256)} %frac_ref.1, ...), custom_call_target="tpu_custom_call" | custom-call | tf_op jit(solution)/shard_map/pallas_call | solution.py:439
  44.7 0.0 copy-start
  44.7 2.3 %copy.17 = f32[1,2048,128]{2,1,0:T(8,128)} copy(f32[1,2048,128]{2,1,0:T(8,128)} %bitcast.8) | data formatting | bytes 2097152
  47.0 0.0 copy-done
  47.0 0.6 %copy.18 = f32[5,256]{1,0:T(8,128)} copy(f32[5,256]{1,0:T(8,128)S(1)} %copy-done) | data formatting | bytes 10240
Async XLA Ops:
  44.7 2.3 %copy-start = (f32[5,256]{1,0:T(8,128)S(1)}, f32[5,256]{1,0:T(8,128)}, u32[]{:S(2)}) copy-start(f32[5,256]{1,0:T(8,128)} %get-tuple-element.9) | copy-start | bytes 15364
where the time goes:
time: 47.8 us; the launch traced here: 47.6 us
  Pallas kernels  42.8 us (90%)
  local copies, waits for them, and re-layouts  2.87 us (6%)
  between operations  1.94 us (4%)
    pallas_call x1, Pallas kernels, body(): pl.pallas_call(functools.partial(kernel, tiles, nband, cap), out_shape=(j...  42.8 us
    unnamed x4, local copies, waits for them, and re-layouts  2.87 us

commit v1 on v0

--- a/solution.py
+++ b/solution.py
@@ -50,19 +50,24 @@
     tiles,
     nband,
     cap,
-    owner_ref,
-    local_ref,
-    weight_ref,
     offset_ref,
     expo_ref,
-    amp_ref,
-    frac_ref,
+    owner_hbm,
+    local_hbm,
+    weight_hbm,
+    amp_hbm,
+    frac_hbm,
     sky_hbm,
     obs_hbm,
     col_hbm,
     rowp_hbm,
     total,
     summed_ref,
+    owner_ref,
+    local_ref,
+    weight_ref,
+    amp_ref,
+    frac_ref,
     sky,
     sky_t,
     obs,
@@ -112,12 +117,21 @@
     comps = blur.shape[0]
     pixels = width * rows
     nblk = width // 256
-    half = tiles // 2
 
     loads = [
         pltpu.make_async_copy(src, dst, load_sem.at[i])
         for i, (src, dst) in enumerate(
-            ((sky_hbm, sky), (obs_hbm, obs), (col_hbm, colp), (rowp_hbm, rowp))
+            (
+                (owner_hbm, owner_ref),
+                (local_hbm, local_ref),
+                (sky_hbm, sky),
+                (obs_hbm, obs),
+                (col_hbm, colp),
+                (rowp_hbm, rowp),
+                (weight_hbm, weight_ref),
+                (amp_hbm, amp_ref),
+                (frac_hbm, frac_ref),
+            )
         )
     ]
     for load in loads:
@@ -183,6 +197,8 @@
         def _():
             arrival(src, dst, send, recv, p).wait_recv()
 
+    loads[0].wait()
+    loads[1].wait()
     owner = owner_ref[...]
     member = jnp.where(iota((tiles, width), 0) == owner, 1.0, 0.0)
     pieces = [member[:, b * 128 : (b + 1) * 128] for b in range(width // 128)]
@@ -213,7 +229,7 @@
         deliver(req_out, req_in, req_s, req_r, p)
 
     loop(0, tiles, ask)
-    loads[0].wait()
+    loads[2].wait()
     for b in range(segs // 128):
         sky_t[:, b * 128 : (b + 1) * 128] = sky[b * 128 : (b + 1) * 128, :].T
 
@@ -233,7 +249,7 @@
 
     loop(0, tiles, serve)
 
-    for load in loads[1:]:
+    for load in loads[3:]:
         load.wait()
     expo = expo_ref[0, 0]
     offset = offset_ref[0, 0]
@@ -324,15 +340,14 @@
             stack.append(part.astype(BF))
         adjoint = dot(tall_all, jnp.concatenate(stack, axis=0))
         adj[:, i * 256 : (i + 1) * 256] = adjoint
-        seg_grad[:, i * 256 : (i + 1) * 256] = dot(interp, adjoint.astype(BF)).astype(BF)
+        seg_grad[i * 256 : (i + 1) * 256, :] = dot(interp, adjoint.astype(BF)).T.astype(BF)
 
     def give(step):
         p = after(step)
-        sent = lax.dot_general(seg_grad[...], hits[p], NT, preferred_element_type=F32)
-        grads_out[p] = sent.astype(BF)
+        grads_out[p] = dot(hits[p], seg_grad[...]).astype(BF)
         deliver(grads_out, grads_in, grads_s, grads_r, p)
 
-    loop(0, half, give)
+    loop(0, tiles, give)
 
     terms = []
     for q in range(comps):
@@ -362,8 +377,6 @@
 
     loop(1, nband, lambda k: swap(k, True).start())
 
-    loop(half, tiles, give)
-
     loop(1, nband, lambda k: swap(k, False).wait_recv())
     expos = summed_ref.shape[1]
     column = iota((8, expos), 1).astype(F32)
@@ -393,7 +406,7 @@
         p = ahead(step)
         receive(grads_out, grads_in, grads_s, grads_r, p)
         chosen = picks[p] if keep else pick(p)
-        total[...] += lax.dot_general(chosen, grads_in[p], NT, preferred_element_type=F32)
+        total[...] += dot(chosen, grads_in[p])
 
     loop(0, tiles, collect)
 
@@ -442,9 +455,14 @@
             jax.ShapeDtypeStruct((segs, rows), F32),
             jax.ShapeDtypeStruct((comps + 1, expos), F32),
         ),
-        in_specs=[vmem, vmem, vmem, smem, smem, smem, smem, hbm, hbm, hbm, hbm],
+        in_specs=[smem] * 2 + [hbm] * 9,
         out_specs=(vmem, vmem),
         scratch_shapes=[
+            pltpu.VMEM((1, width), jnp.int32),
+            pltpu.VMEM((1, width), jnp.int32),
+            pltpu.VMEM((1, rows), F32),
+            pltpu.SMEM((comps, expos), F32),
+            pltpu.SMEM((expos,), F32),
             pltpu.VMEM((segs, rows), BF),
             pltpu.VMEM((rows, segs), BF),
             pltpu.VMEM((width, rows), BF),
@@ -456,8 +474,8 @@
             pltpu.VMEM((tiles, 1, cap), F32),
             pltpu.VMEM((tiles, rows, cap), BF),
             pltpu.VMEM((tiles, rows, cap), BF),
-            pltpu.VMEM((tiles, rows, cap), BF),
-            pltpu.VMEM((tiles, rows, cap), BF),
+            pltpu.VMEM((tiles, cap, rows), BF),
+            pltpu.VMEM((tiles, cap, rows), BF),
             pltpu.VMEM((8, 128), F32),
             pltpu.VMEM((nband, 8, 128), F32),
             pltpu.VMEM((8, expos), F32),
@@ -474,8 +492,8 @@
             pltpu.VMEM((rows, width + 256), BF),
             pltpu.VMEM((comps, rows, width), F32),
             pltpu.VMEM((rows, width), F32),
-            pltpu.VMEM((rows, width), BF),
-            dma((4,)),
+            pltpu.VMEM((width, rows), BF),
+            dma((9,)),
         ]
         + [dma((tiles,))] * 6
         + [dma((nband,))] * 2
@@ -484,11 +502,11 @@
             collective_id=0, has_side_effects=True, vmem_limit_bytes=60 * 1024 * 1024
         ),
     )(
+        row_offset,
+        exposure_of,
         foot_owner.reshape(1, width),
         foot_local.reshape(1, width),
         row_weight.reshape(1, rows),
-        row_offset,
-        exposure_of,
         amplitude,
         subpixel_shift,
         sky_model[0],

time: 47.8 us -> 46.9 us (0.981)
  Pallas kernels: 42.8 us -> 41.9 us
    pallas_call x1, Pallas kernels: 42.8 us -> 41.9 us  [body(): pl.pallas_call(functools.partial(kernel, tiles, nband, cap), out_shape=(j...]
where the time goes in v1:
time: 46.9 us; the launch traced here: 46.7 us
  Pallas kernels  41.9 us (89%)
  local copies, waits for them, and re-layouts  2.87 us (6%)
  between operations  1.94 us (4%)
    pallas_call x1, Pallas kernels, body(): pl.pallas_call(functools.partial(kernel, tiles, nband, cap), out_shape=(j...  41.9 us
    unnamed x4, local copies, waits for them, and re-layouts  2.87 us

profile of v1, /device:TPU:0, one launch (start us, length us, event | category | flops | bytes accessed | tf_op | source)
XLA Modules:
  0.0 46.7 jit_solution(13877192532324743253)
XLA Ops:
  1.9 41.9 %shard_map.122 = (f32[2048,128]{1,0:T(8,128)}, f32[5,256]{1,0:T(8,128)}) custom-call(s32[1,1]{1,0:T(1,128)S(6)} %copy.15.offset_ref, s32[1,1]{1,0:T(1,128)S(6)} %copy.16.expo_ref, s32[1,1024]{1,0:T(1,128)} %bitcast.13, s32[1,1024]{1,0:T(1,128)} %bitcast.14, f32[1,128]{1,0:T(1,128)} %bitcast.15, f32[4,256]{1,0:T(4,128)} %amp_hbm.1, f32[256]{0:T(256)} %frac_hbm.1, ...), custom_call_target="tpu_custom_call" | custom-call | tf_op jit(solution)/shard_map/pallas_call | solution.py:452
  43.8 0.0 copy-start
  43.9 2.3 %copy.17 = f32[1,2048,128]{2,1,0:T(8,128)} copy(f32[1,2048,128]{2,1,0:T(8,128)} %bitcast.8) | data formatting | bytes 2097152
  46.1 0.0 copy-done
  46.1 0.6 %copy.18 = f32[5,256]{1,0:T(8,128)} copy(f32[5,256]{1,0:T(8,128)S(1)} %copy-done) | data formatting | bytes 10240
Async XLA Ops:
  43.8 2.3 %copy-start = (f32[5,256]{1,0:T(8,128)S(1)}, f32[5,256]{1,0:T(8,128)}, u32[]{:S(2)}) copy-start(f32[5,256]{1,0:T(8,128)} %get-tuple-element.9) | copy-start | bytes 15364

commit v2 on v1

--- a/solution.py
+++ b/solution.py
@@ -61,7 +61,7 @@
     obs_hbm,
     col_hbm,
     rowp_hbm,
-    total,
+    grad_hbm,
     summed_ref,
     owner_ref,
     local_ref,
@@ -98,7 +98,9 @@
     back,
     adj,
     seg_grad,
+    total,
     load_sem,
+    store_sem,
     req_s,
     req_r,
     rows_s,
@@ -307,7 +309,7 @@
     fet[...] = jnp.zeros_like(fet)
 
     def take(step):
-        p = after(step)
+        p = lax.rem(me + step, tiles)
         receive(rows_out, rows_in, rows_s, rows_r, p)
         fet[...] += dot(rows_in[p], hits[p])
 
@@ -403,12 +405,26 @@
     total[...] = jnp.zeros_like(total)
 
     def collect(step):
-        p = ahead(step)
+        p = lax.rem(me + tiles - step, tiles)
         receive(grads_out, grads_in, grads_s, grads_r, p)
         chosen = picks[p] if keep else pick(p)
         total[...] += dot(chosen, grads_in[p])
 
-    loop(0, tiles, collect)
+    loop(0, tiles - 1, collect)
+    last = lax.rem(me + 1, tiles)
+    arrival(grads_out, grads_in, grads_s, grads_r, last).wait_recv()
+    chosen = None if keep else pick(last)
+    stores = []
+    size = segs // 4
+    for i in range(4):
+        at = slice(i * size, (i + 1) * size)
+        total[at, :] += dot(picks[last, at, :] if keep else chosen[at], grads_in[last])
+        stores.append(
+            pltpu.make_async_copy(
+                total.at[pl.ds(i * size, size)], grad_hbm.at[pl.ds(i * size, size)], store_sem.at[i]
+            )
+        )
+        stores[-1].start()
 
     loop(1, tiles, lambda k: tell(k, False).wait_recv())
     summed = lax.fori_loop(0, tiles, lambda t, acc: acc + part_in[t], jnp.zeros((8, expos), F32))
@@ -423,6 +439,8 @@
 
     loop(1, tiles, settle)
     loop(1, nband, lambda k: swap(k, True).wait_send())
+    for store in stores:
+        store.wait()
 
 
 def body(
@@ -456,7 +474,7 @@
             jax.ShapeDtypeStruct((comps + 1, expos), F32),
         ),
         in_specs=[smem] * 2 + [hbm] * 9,
-        out_specs=(vmem, vmem),
+        out_specs=(hbm, vmem),
         scratch_shapes=[
             pltpu.VMEM((1, width), jnp.int32),
             pltpu.VMEM((1, width), jnp.int32),
@@ -493,7 +511,9 @@
             pltpu.VMEM((comps, rows, width), F32),
             pltpu.VMEM((rows, width), F32),
             pltpu.VMEM((width, rows), BF),
+            pltpu.VMEM((segs, rows), F32),
             dma((9,)),
+            dma((4,)),
         ]
         + [dma((tiles,))] * 6
         + [dma((nband,))] * 2

time: 46.9 us -> 46.4 us (0.989)
  Pallas kernels: 41.9 us -> 41.4 us
    pallas_call x1, Pallas kernels: 41.9 us -> 41.4 us  [body(): pl.pallas_call(functools.partial(kernel, tiles, nband, cap), out_shape=(j...]
where the time goes in v2:
time: 46.4 us; the launch traced here: 46.2 us
  Pallas kernels  41.4 us (89%)
  local copies, waits for them, and re-layouts  2.87 us (6%)
  between operations  1.94 us (4%)
    pallas_call x1, Pallas kernels, body(): pl.pallas_call(functools.partial(kernel, tiles, nband, cap), out_shape=(j...  41.4 us
    unnamed x4, local copies, waits for them, and re-layouts  2.87 us

profile of v2, /device:TPU:0, one launch (start us, length us, event | category | flops | bytes accessed | tf_op | source)
XLA Modules:
  0.0 46.2 jit_solution(12711150854075144929)
XLA Ops:
  1.9 41.4 %shard_map.122 = (f32[2048,128]{1,0:T(8,128)}, f32[5,256]{1,0:T(8,128)}) custom-call(s32[1,1]{1,0:T(1,128)S(6)} %copy.15.offset_ref, s32[1,1]{1,0:T(1,128)S(6)} %copy.16.expo_ref, s32[1,1024]{1,0:T(1,128)} %bitcast.13, s32[1,1024]{1,0:T(1,128)} %bitcast.14, f32[1,128]{1,0:T(1,128)} %bitcast.15, f32[4,256]{1,0:T(4,128)} %amp_hbm.1, f32[256]{0:T(256)} %frac_hbm.1, ...), custom_call_target="tpu_custom_call" | custom-call | tf_op jit(solution)/shard_map/pallas_call | solution.py:470
  43.3 0.0 copy-start
  43.3 2.3 %copy.17 = f32[1,2048,128]{2,1,0:T(8,128)} copy(f32[1,2048,128]{2,1,0:T(8,128)} %bitcast.8) | data formatting | bytes 2097152
  45.6 0.0 copy-done
  45.6 0.6 %copy.18 = f32[5,256]{1,0:T(8,128)} copy(f32[5,256]{1,0:T(8,128)S(1)} %copy-done) | data formatting | bytes 10240
Async XLA Ops:
  43.3 2.3 %copy-start = (f32[5,256]{1,0:T(8,128)S(1)}, f32[5,256]{1,0:T(8,128)}, u32[]{:S(2)}) copy-start(f32[5,256]{1,0:T(8,128)} %get-tuple-element.9) | copy-start | bytes 15364
